TPU v7x, 32 devices: a whole 2x2x4 slice. The times are simulated.
32 devices in a mesh: group: 8 (over z, y), tp: 4 (over x, core).
Axes of the slice: x: 2, y: 2, z: 4, core: 2. Of those that a mesh axis runs over, the one named last changes fastest.
Arguments:
- pf_query: bfloat16 [2048, 8192], P('group', 'tp'), may hold values from -16 to 16
- pf_cache: bfloat16 [8, 2, 4096, 1024], P('group', None, 'tp'), may hold values from -16 to 16
- pf_offset: int32 [8], replicated, may hold values from 0 to 3840
- dec_query: bfloat16 [16, 8192], P('group', 'tp'), may hold values from -16 to 16
- dec_cache: bfloat16 [24, 2, 2048, 1024], P('group', None, 'tp'), may hold values from -16 to 16
- slot_owner: int32 [24], replicated, may hold values from 0 to 15, as said below
- slot_len: int32 [24], replicated, may hold values from 1 to 2048
Outputs:
- pf_out: bfloat16 [2048, 8192], P('group', 'tp')
- dec_out: bfloat16 [16, 8192], P('group', 'tp')
Inputs may be any that keep to these rules, and one draw needn't show every extreme that they name: `slot_owner`: every decode request owns one or two slots.
All inputs are finite; a program needn't handle non-finite values.
Results may differ from a plain program's by a relative error of at most 0.005.
Values may be sent and summed in bfloat16 or wider, within the bound.
A program may use at most 128 MiB of HBM per device.

v0:
```python
import jax
import jax.numpy as jnp
from jax import lax
from jax.sharding import PartitionSpec as P

QH = 64
KVH = 8
HD = 128
negative_big = -1e30


def merged_2(value, axis, join):
    pieces = jax.tree.map(lambda part: lax.all_gather(part, axis), value)
    head = jax.tree.map(lambda part: part[0], pieces)
    tail = jax.tree.map(lambda part: part[1:], pieces)
    running, _ = lax.scan(lambda running, share: (join(running, share), None), head, tail)
    return running


def attend_block(queries, cache_keys, cache_values, visible, score_scale):
    scores = (
        jnp.einsum("qgd,nd->gqn", queries, cache_keys, preferred_element_type=jnp.float32)
        * score_scale
    )
    scores = jnp.where(visible[None], scores, negative_big)
    maxima = jnp.max(scores, axis=-1)
    weights = jnp.where(visible[None], jnp.exp(scores - maxima[..., None]), 0.0).astype(
        jnp.bfloat16
    )
    totals = jnp.sum(weights, axis=-1, dtype=jnp.float32)
    weighted = jnp.einsum("gqn,nd->gqd", weights, cache_values, preferred_element_type=jnp.float32)
    return (maxima, totals, weighted)


def merge_along(maxima, totals, weighted, axis):
    largest = jnp.max(maxima, axis=axis, keepdims=True)
    factor = jnp.exp(maxima - largest)
    return (
        jnp.squeeze(largest, axis),
        jnp.sum(totals * factor, axis=axis),
        jnp.sum(weighted * factor[..., None], axis=axis),
    )


def combine_pair(first, second):
    largest = jnp.maximum(first[0], second[0])
    first_factor = jnp.exp(first[0] - largest)
    second_factor = jnp.exp(second[0] - largest)
    return (
        largest,
        first[1] * first_factor + second[1] * second_factor,
        first[2] * first_factor[..., None] + second[2] * second_factor[..., None],
    )


def masked_merge(hits, maxima, totals, weighted):
    selected_picks = jnp.where(hits[:, :, None], maxima[None], negative_big)
    largest = jnp.max(selected_picks, axis=1)
    factor = jnp.where(hits[:, :, None], jnp.exp(selected_picks - largest[:, None]), 0.0)
    denominator = jnp.einsum("abh,bh->ah", factor, totals, precision=lax.Precision.HIGHEST)
    numerator = jnp.einsum("abh,bhd->ahd", factor, weighted, precision=lax.Precision.HIGHEST)
    return (largest, denominator, numerator)


def on_device(pf_query, pf_cache, pf_offset, dec_query, dec_cache, slot_owner, slot_len):
    tp_count = lax.axis_size("tp")
    tp_rank = lax.axis_index("tp")
    group_rank = lax.axis_index("group")
    head_size = HD
    kv_heads = KVH
    width = QH // KVH
    local_heads = QH // tp_count
    score_scale = head_size ** (-0.5)
    pf_rows = pf_query.shape[0]
    local_len = pf_cache.shape[2]
    offset = lax.dynamic_index_in_dim(pf_offset, group_rank, keepdims=False)
    query_pos = offset + jnp.arange(pf_rows, dtype=jnp.int32)
    every_head = lax.all_gather(pf_query, "tp", axis=1, tiled=True)
    grouped = jnp.moveaxis(every_head.reshape(pf_rows, kv_heads, width, head_size), 1, 0)
    cache_keys = jnp.moveaxis(pf_cache[0, 0].reshape(local_len, kv_heads, head_size), 1, 0)
    cache_values = jnp.moveaxis(pf_cache[0, 1].reshape(local_len, kv_heads, head_size), 1, 0)
    key_pos = tp_rank * local_len + jnp.arange(local_len, dtype=jnp.int32)
    visible = key_pos[None, :] <= query_pos[:, None]
    maxima, totals, weighted = lax.map(
        lambda items: attend_block(items[0], items[1], items[2], visible, score_scale),
        (grouped, cache_keys, cache_values),
    )
    maxima = maxima.reshape(tp_count, local_heads, pf_rows)
    totals = totals.reshape(tp_count, local_heads, pf_rows)
    weighted = weighted.reshape(tp_count, local_heads, pf_rows, head_size)
    maxima, totals, weighted = (
        lax.all_to_all(maxima, "tp", split_axis=0, concat_axis=0, tiled=True),
        lax.all_to_all(totals, "tp", split_axis=0, concat_axis=0, tiled=True),
        lax.all_to_all(weighted, "tp", split_axis=0, concat_axis=0, tiled=True),
    )
    largest, denominator, numerator = merge_along(maxima, totals, weighted, 0)
    prefill_heads = numerator / denominator[..., None]
    pf_out = (
        jnp.moveaxis(prefill_heads, 1, 0)
        .reshape(pf_rows, local_heads * head_size)
        .astype(jnp.bfloat16)
    )
    served = dec_query.shape[0]
    head_queries_dec = lax.all_gather(dec_query, "tp", axis=1, tiled=True)
    all_queries = lax.all_gather(head_queries_dec, "group", axis=0, tiled=True)
    slots_here = dec_cache.shape[0]
    slot_local_len = dec_cache.shape[2]
    owners = lax.dynamic_slice_in_dim(slot_owner, group_rank * slots_here, slots_here)
    length_list = lax.dynamic_slice_in_dim(slot_len, group_rank * slots_here, slots_here)
    slot_queries = jnp.take(all_queries, owners, axis=0).reshape(
        slots_here, kv_heads, width, head_size
    )
    slot_keys = dec_cache[:, 0].reshape(slots_here, slot_local_len, kv_heads, head_size)
    slot_values = dec_cache[:, 1].reshape(slots_here, slot_local_len, kv_heads, head_size)
    scores = (
        jnp.einsum("skgd,slkd->skgl", slot_queries, slot_keys, preferred_element_type=jnp.float32)
        * score_scale
    )
    slot_pos = tp_rank * slot_local_len + jnp.arange(slot_local_len, dtype=jnp.int32)
    live = (slot_pos[None, :] < length_list[:, None])[:, None, None, :]
    scores = jnp.where(live, scores, negative_big)
    slot_max = jnp.max(scores, axis=-1)
    slot_weights = jnp.where(live, jnp.exp(scores - slot_max[..., None]), 0.0).astype(jnp.bfloat16)
    slot_totals = jnp.sum(slot_weights, axis=-1, dtype=jnp.float32)
    slot_weighted = jnp.einsum(
        "skgl,slkd->skgd", slot_weights, slot_values, preferred_element_type=jnp.float32
    )
    slot_max = slot_max.reshape(slots_here, QH)
    slot_totals = slot_totals.reshape(slots_here, QH)
    slot_weighted = slot_weighted.reshape(slots_here, QH, head_size)
    merged = merged_2((slot_max, slot_totals, slot_weighted), "tp", combine_pair)
    head_max = lax.dynamic_slice_in_dim(merged[0], tp_rank * local_heads, local_heads, 1)
    head_totals = lax.dynamic_slice_in_dim(merged[1], tp_rank * local_heads, local_heads, 1)
    head_weighted = lax.dynamic_slice_in_dim(merged[2], tp_rank * local_heads, local_heads, 1)
    every_max, every_totals, every_weighted = (
        lax.all_gather(head_max, "group", axis=0, tiled=True),
        lax.all_gather(head_totals, "group", axis=0, tiled=True),
        lax.all_gather(head_weighted, "group", axis=0, tiled=True),
    )
    mine = group_rank * served + jnp.arange(served, dtype=jnp.int32)
    hits = slot_owner[None, :] == mine[:, None]
    largest_dec, denominator_dec, numerator_dec = masked_merge(
        hits, every_max, every_totals, every_weighted
    )
    dec_out = (
        (numerator_dec / denominator_dec[..., None])
        .reshape(served, local_heads * head_size)
        .astype(jnp.bfloat16)
    )
    return (pf_out, dec_out)


def solution(mesh):
    placed = (
        P("group", "tp"),
        P("group", None, "tp", None),
        P(),
        P("group", "tp"),
        P("group", None, "tp", None),
        P(),
        P(),
    )
    return jax.shard_map(
        on_device,
        mesh=mesh,
        in_specs=placed,
        out_specs=(P("group", "tp"), P("group", "tp")),
        check_vma=False,
    )
```

profile of v0, /device:TPU:0, one launch (start us, length us, event | category | flops | bytes accessed | tf_op | source)
XLA Modules:
  0.0 403.5 jit_solution(4472428663473686276)
XLA Ops:
  7.2 2.3 copy.40
  9.5 4.0 fusion.46
  13.5 4.0 copy.61
  17.5 2.6 copy.62
  21.2 26.1 %all-gather.5.cloned.1.call-done = bf16[256,8192]{0,1:T(8,128)(2,1)} async-done(((bf16[256,2048]{0,1:T(8,128)(2,1)}), bf16[256,8192]{0,1:T(8,128)(2,1)}) %all-gather.5.cloned.1.call-update) | async-done | bytes 4194320 | tf_op jit(solution)/shard_map/all_gather | solution.py:78
  47.3 74.8 %while.30 = (s32[]{:T(128)}, f32[8,8,256]{2,1,0:T(8,128)S(1)}, f32[8,8,256]{2,1,0:T(8,128)S(1)}, f32[8,8,256,128]{3,2,1,0:T(8,128)}, bf16[8,1024,128]{1,2,0:T(8,...) while((s32[]{:T(128)}, f32[8,8,256]{2,1,0:T(8,128)S(1)}, ...), condition=%wide.region_3.4_spmd.clone, body=%wide.region_0.3_spmd.clone.sunk | while | flops 1105457152 | bytes 28384368 | solution.py:84
  47.6 2.6 fusion.59
  50.2 2.0 convert_reduce_fusion.3
  52.2 4.6 %fusion.60 = f32[8,8,256,128]{3,2,1,0:T(8,128)} fusion(f32[8,8,256,128]{3,2,1,0:T(8,128)} %get-tuple-element.319, s32[]{:T(128)S(6)} %copy.81, bf16[8,1024,128]{1,2,0:T(8,128)(2,1)} %get-tuple-element.332, f32[1024,256,8]{1,0,2:T(8,128)S(1)} %get-tuple-element.303, f32[8,256]{1,0:T(8,128)S(1)} %get-tuple-element.302, ...), kind=kOutput, calls=%fused_computation.15.clone.1 | convolution fusion | flops 547356672 | bytes 9970688 | tf_op jit(solution)/shard_map/while/body/eval_jaxpr/gqn,nd->gqd/dot_general | solution.py:31
  57.0 2.6 fusion.59
  59.6 2.0 convert_reduce_fusion.3
  61.6 4.5 %fusion.60 = f32[8,8,256,128]{3,2,1,0:T(8,128)} fusion(f32[8,8,256,128]{3,2,1,0:T(8,128)} %get-tuple-element.319, s32[]{:T(128)S(6)} %copy.81, bf16[8,1024,128]{1,2,0:T(8,128)(2,1)} %get-tuple-element.332, f32[1024,256,8]{1,0,2:T(8,128)S(1)} %get-tuple-element.303, f32[8,256]{1,0:T(8,128)S(1)} %get-tuple-element.302, ...), kind=kOutput, calls=%fused_computation.15.clone.1 | convolution fusion | flops 547356672 | bytes 9970688 | tf_op jit(solution)/shard_map/while/body/eval_jaxpr/gqn,nd->gqd/dot_general | solution.py:31
  66.3 2.6 fusion.59
  68.9 2.0 convert_reduce_fusion.3
  70.9 4.5 %fusion.60 = f32[8,8,256,128]{3,2,1,0:T(8,128)} fusion(f32[8,8,256,128]{3,2,1,0:T(8,128)} %get-tuple-element.319, s32[]{:T(128)S(6)} %copy.81, bf16[8,1024,128]{1,2,0:T(8,128)(2,1)} %get-tuple-element.332, f32[1024,256,8]{1,0,2:T(8,128)S(1)} %get-tuple-element.303, f32[8,256]{1,0:T(8,128)S(1)} %get-tuple-element.302, ...), kind=kOutput, calls=%fused_computation.15.clone.1 | convolution fusion | flops 547356672 | bytes 9970688 | tf_op jit(solution)/shard_map/while/body/eval_jaxpr/gqn,nd->gqd/dot_general | solution.py:31
  75.6 2.6 fusion.59
  78.2 2.0 convert_reduce_fusion.3
  80.3 4.5 %fusion.60 = f32[8,8,256,128]{3,2,1,0:T(8,128)} fusion(f32[8,8,256,128]{3,2,1,0:T(8,128)} %get-tuple-element.319, s32[]{:T(128)S(6)} %copy.81, bf16[8,1024,128]{1,2,0:T(8,128)(2,1)} %get-tuple-element.332, f32[1024,256,8]{1,0,2:T(8,128)S(1)} %get-tuple-element.303, f32[8,256]{1,0:T(8,128)S(1)} %get-tuple-element.302, ...), kind=kOutput, calls=%fused_computation.15.clone.1 | convolution fusion | flops 547356672 | bytes 9970688 | tf_op jit(solution)/shard_map/while/body/eval_jaxpr/gqn,nd->gqd/dot_general | solution.py:31
  84.9 2.6 fusion.59
  87.5 2.0 convert_reduce_fusion.3
  89.6 4.5 %fusion.60 = f32[8,8,256,128]{3,2,1,0:T(8,128)} fusion(f32[8,8,256,128]{3,2,1,0:T(8,128)} %get-tuple-element.319, s32[]{:T(128)S(6)} %copy.81, bf16[8,1024,128]{1,2,0:T(8,128)(2,1)} %get-tuple-element.332, f32[1024,256,8]{1,0,2:T(8,128)S(1)} %get-tuple-element.303, f32[8,256]{1,0:T(8,128)S(1)} %get-tuple-element.302, ...), kind=kOutput, calls=%fused_computation.15.clone.1 | convolution fusion | flops 547356672 | bytes 9970688 | tf_op jit(solution)/shard_map/while/body/eval_jaxpr/gqn,nd->gqd/dot_general | solution.py:31
  94.3 2.6 fusion.59
  96.9 2.0 convert_reduce_fusion.3
  99.0 4.5 %fusion.60 = f32[8,8,256,128]{3,2,1,0:T(8,128)} fusion(f32[8,8,256,128]{3,2,1,0:T(8,128)} %get-tuple-element.319, s32[]{:T(128)S(6)} %copy.81, bf16[8,1024,128]{1,2,0:T(8,128)(2,1)} %get-tuple-element.332, f32[1024,256,8]{1,0,2:T(8,128)S(1)} %get-tuple-element.303, f32[8,256]{1,0:T(8,128)S(1)} %get-tuple-element.302, ...), kind=kOutput, calls=%fused_computation.15.clone.1 | convolution fusion | flops 547356672 | bytes 9970688 | tf_op jit(solution)/shard_map/while/body/eval_jaxpr/gqn,nd->gqd/dot_general | solution.py:31
  103.7 2.6 fusion.59
  106.3 2.0 convert_reduce_fusion.3
  108.3 4.5 %fusion.60 = f32[8,8,256,128]{3,2,1,0:T(8,128)} fusion(f32[8,8,256,128]{3,2,1,0:T(8,128)} %get-tuple-element.319, s32[]{:T(128)S(6)} %copy.81, bf16[8,1024,128]{1,2,0:T(8,128)(2,1)} %get-tuple-element.332, f32[1024,256,8]{1,0,2:T(8,128)S(1)} %get-tuple-element.303, f32[8,256]{1,0:T(8,128)S(1)} %get-tuple-element.302, ...), kind=kOutput, calls=%fused_computation.15.clone.1 | convolution fusion | flops 547356672 | bytes 9970688 | tf_op jit(solution)/shard_map/while/body/eval_jaxpr/gqn,nd->gqd/dot_general | solution.py:31
  113.0 2.6 fusion.59
  115.6 2.0 convert_reduce_fusion.3
  117.6 4.5 %fusion.60 = f32[8,8,256,128]{3,2,1,0:T(8,128)} fusion(f32[8,8,256,128]{3,2,1,0:T(8,128)} %get-tuple-element.319, s32[]{:T(128)S(6)} %copy.81, bf16[8,1024,128]{1,2,0:T(8,128)(2,1)} %get-tuple-element.332, f32[1024,256,8]{1,0,2:T(8,128)S(1)} %get-tuple-element.303, f32[8,256]{1,0:T(8,128)S(1)} %get-tuple-element.302, ...), kind=kOutput, calls=%fused_computation.15.clone.1 | convolution fusion | flops 547356672 | bytes 9970688 | tf_op jit(solution)/shard_map/while/body/eval_jaxpr/gqn,nd->gqd/dot_general | solution.py:31
  122.1 7.1 %all_to_all.15 = f32[4,16,256]{2,1,0:T(8,128)} all-to-all(f32[4,16,256]{2,1,0:T(8,128)S(1)} %bitcast.139), channel_id=1, replica_groups=mesh['group'=8,'tp'=4] {'tp'}, dimensions={0} | all-to-all | bytes 131072 | tf_op jit(solution)/shard_map/all_to_all | solution.py:93
  129.2 7.1 %all_to_all.16 = f32[4,16,256]{2,1,0:T(8,128)} all-to-all(f32[4,16,256]{2,1,0:T(8,128)S(1)} %bitcast.138), channel_id=1, replica_groups=mesh['group'=8,'tp'=4] {'tp'}, dimensions={0} | all-to-all | bytes 131072 | tf_op jit(solution)/shard_map/all_to_all | solution.py:92
  136.4 5.7 %all-to-all-start = ((f32[4,16,256,128]{3,2,1,0:T(8,128)}), f32[4,16,256,128]{3,2,1,0:T(8,128)}, u32[]{:S(2)}, u32[]{:S(2)}) async-start(f32[4,16,256,128]{3,2,1,0:T(8,128)} %bitcast.130), calls=%async_computation | async-start | bytes 16777216 | tf_op jit(solution)/shard_map/all_to_all | solution.py:94
  142.1 6.9 %fusion.45 = (bf16[3,1,512,1024]{3,2,1,0:T(8,128)(2,1)}, bf16[3,1,512,1024]{3,2,1,0:T(8,128)(2,1)}) fusion(bf16[3,2,512,1024]{3,2,1,0:T(8,128)(2,1)} %param.15), kind=kLoop, calls=%fused_computation.81 | loop fusion | bytes 12582912 | tf_op jit(solution)/shard_map/slice | solution.py:114
  149.0 3.2 copy.63
  152.2 84.0 %all_gather.28 = bf16[2,8192]{1,0:T(2,128)(2,1)S(1)} all-gather(bf16[2,2048]{1,0:T(2,128)(2,1)S(1)} %copy-done.2), channel_id=1, replica_groups=mesh['group'=8,'tp'=4] {'tp'}, dimensions={1}, use_global_device_ids=true | all-gather | bytes 40960 | tf_op jit(solution)/shard_map/all_gather | solution.py:104
  236.2 32.8 %all-gather = bf16[8,2,8192]{2,1,0:T(2,128)(2,1)} all-gather(bf16[1,2,8192]{2,1,0:T(2,128)(2,1)S(1)} %bitcast.136), channel_id=1, replica_groups=mesh['group'=8,'tp'=4] {'group'}, dimensions={0}, use_global_device_ids=true | all-gather | bytes 294912 | tf_op jit(solution)/shard_map/all_gather | solution.py:105
  269.0 1.0 reshape.122
  270.7 1.2 gather_fusion
  272.0 1.5 fusion.47
  273.5 0.7 all_gather_reshape.9
  274.4 0.7 all_gather_reshape.10
  275.1 3.2 copy.64
  278.3 5.3 %all_gather.30 = f32[4,3,64]{2,1,0:T(4,128)S(1)} all-gather(f32[1,3,64]{2,1,0:T(4,128)} %all_gather_reshape.9), channel_id=1, replica_groups=mesh['group'=8,'tp'=4] {'tp'}, dimensions={0}, use_global_device_ids=true | all-gather | bytes 3840 | tf_op jit(solution)/shard_map/all_gather | solution.py:13
  284.2 5.3 %all_gather.31 = f32[4,3,64]{2,1,0:T(4,128)S(1)} all-gather(f32[1,3,64]{2,1,0:T(4,128)} %all_gather_reshape.10), channel_id=1, replica_groups=mesh['group'=8,'tp'=4] {'tp'}, dimensions={0}, use_global_device_ids=true | all-gather | bytes 3840 | tf_op jit(solution)/shard_map/all_gather | solution.py:13
  289.4 0.6 slice.46
  290.0 1.0 convolution_bitcast_fusion.1
  291.0 6.5 %all_gather.32 = f32[4,3,64,128]{3,2,1,0:T(8,128)S(1)} all-gather(f32[1,3,64,128]{3,2,1,0:T(8,128)S(1)} %convolution_bitcast_fusion.1), channel_id=1, replica_groups=mesh['group'=8,'tp'=4] {'tp'}, dimensions={0}, use_global_device_ids=true | all-gather | bytes 491520 | tf_op jit(solution)/shard_map/all_gather | solution.py:13
  297.6 0.7 slice_bitcast_fusion.2
  298.3 0.7 slice_bitcast_fusion.1
  298.9 2.6 while.29
  299.0 0.7 fusion.56
  299.8 0.7 fusion.56
  300.7 0.7 fusion.56
  301.6 26.0 %all-gather.2 = f32[8,3,16]{2,1,0:T(4,128)S(1)} all-gather(f32[1,3,16]{2,1,0:T(4,128)S(1)} %dynamic-slice_bitcast_fusion), channel_id=1, replica_groups=mesh['group'=8,'tp'=4] {'group'}, dimensions={0}, use_global_device_ids=true | all-gather | bytes 1728 | tf_op jit(solution)/shard_map/all_gather | solution.py:137
  327.8 26.2 %all-gather.1 = f32[8,3,16]{2,1,0:T(4,128)S(1)} all-gather(f32[1,3,16]{2,1,0:T(4,128)S(1)} %dynamic-slice_bitcast_fusion.1), channel_id=1, replica_groups=mesh['group'=8,'tp'=4] {'group'}, dimensions={0}, use_global_device_ids=true | all-gather | bytes 1728 | tf_op jit(solution)/shard_map/all_gather | solution.py:136
  354.0 30.6 %all_gather.33 = f32[24,16,128]{2,1,0:T(8,128)S(1)} all-gather(f32[3,16,128]{2,1,0:T(8,128)S(1)} %constant_dynamic-slice_fusion), channel_id=1, replica_groups=mesh['group'=8,'tp'=4] {'group'}, dimensions={0}, use_global_device_ids=true | all-gather | bytes 221184 | tf_op jit(solution)/shard_map/all_gather | solution.py:138
  384.7 0.7 broadcast_compare_fusion.2
  385.8 1.0 fusion.20
  386.8 0.8 reduce_max.36
  387.6 0.9 multiply_reduce_fusion.1
  388.5 5.4 %multiply_reduce_fusion = f32[16,256,128]{2,1,0:T(8,128)S(1)} fusion(f32[4,16,256,128]{3,2,1,0:T(8,128)} %all-to-all-done, f32[4,16,256]{2,1,0:T(8,128)S(1)} %get-tuple-element.181), kind=kLoop, calls=%fused_computation.28 | loop fusion | flops 3670016 | bytes 10551296 | tf_op jit(solution)/shard_map/reduce_sum | solution.py:41
  393.9 0.7 fusion.16
  395.2 1.4 copy.52
  (60 shorter events, 6.2 us)
Async XLA Ops:
  7.2 40.2 %all-gather.5.cloned.1.call-start = ((), (), s32[]{:S(2)}) async-start(), calls=%async_computation.3 | async-start | bytes 5242880 | tf_op jit(solution)/shard_map/all_gather | solution.py:78
  13.5 6.5 %copy-start.4 = (s32[8]{0:T(128)S(1)}, s32[8]{0:T(128)}, u32[]{:S(2)}) copy-start(s32[8]{0:T(128)} %param.13) | copy-start | bytes 100
  136.4 252.1 %all-to-all-start = ((f32[4,16,256,128]{3,2,1,0:T(8,128)}), f32[4,16,256,128]{3,2,1,0:T(8,128)}, u32[]{:S(2)}, u32[]{:S(2)}) async-start(f32[4,16,256,128]{3,2,1,0:T(8,128)} %bitcast.130), calls=%async_computation | async-start | bytes 16777216 | tf_op jit(solution)/shard_map/all_to_all | solution.py:94
  149.0 3.2 copy-start.2
  149.0 121.1 %copy-start.5 = (s32[24]{0:T(128)S(1)}, s32[24]{0:T(128)}, u32[]{:S(2)}) copy-start(s32[24]{0:T(128)} %param.17) | copy-start | bytes 292
  149.0 121.2 %copy-start.3 = (s32[24]{0:T(128)S(1)}, s32[24]{0:T(128)}, u32[]{:S(2)}) copy-start(s32[24]{0:T(128)} %param.16) | copy-start | bytes 292
  283.6 6.5 %copy-start = (f32[4,3,64]{2,1,0:T(4,128)}, f32[4,3,64]{2,1,0:T(4,128)S(1)}, u32[]{:S(2)}) copy-start(f32[4,3,64]{2,1,0:T(4,128)S(1)} %all_gather.30) | copy-start | bytes 9220
  289.4 0.6 copy-start.1
Sparse Core Ops, SparseCore 0:
  10.1 37.1 all-gather.4
where the time goes:
time: 405 us; the launch traced here: 403 us
  blocking collectives  231 us (57%)
  matrix products  60.3 us (15%)
  local copies, waits for them, and re-layouts  35.3 us (9%)
  other arithmetic  30.4 us (8%)
  waiting for transfers between devices  26.1 us (6%)
  between operations  14.2 us (4%)
  starting transfers between devices  5.69 us (1%)
    all_gather x1, blocking collectives, on_device(): head_queries_dec = lax.all_gather(dec_query, 'tp', axis=1, tiled=True)  84 us
    dot_general x8, matrix products, attend_block(): jnp.einsum('gqn,nd->gqd', weights, cache_values, preferred_element_type=j...  35.9 us
    all_gather x1, blocking collectives, on_device(): all_queries = lax.all_gather(head_queries_dec, 'group', axis=0, tiled=True)  32.8 us
    all_gather x1, blocking collectives, on_device(): lax.all_gather(head_weighted, 'group', axis=0, tiled=True)  30.6 us
    all_gather x1, blocking collectives, on_device(): lax.all_gather(head_max, 'group', axis=0, tiled=True)  26.2 us
    all_gather x1, waiting for transfers between devices, on_device(): every_head = lax.all_gather(pf_query, 'tp', axis=1, tiled=True)  26.1 us
    all_gather x1, blocking collectives, on_device(): lax.all_gather(head_totals, 'group', axis=0, tiled=True)  26 us
    dot_general x8, matrix products, attend_block(): jnp.einsum('qgd,nd->gqn', queries, cache_keys, preferred_element_type=jnp...  20.8 us
  transfers between devices with their start and end apart: 2, of which 1 were waited for; matrix products, arithmetic and copies ran while one was open for 10% of the time, Pallas kernels for 0%

commit v1 on v0

--- a/solution.py
+++ b/solution.py
@@ -102,7 +102,18 @@
     )
     served = dec_query.shape[0]
     head_queries_dec = lax.all_gather(dec_query, "tp", axis=1, tiled=True)
-    all_queries = lax.all_gather(head_queries_dec, "group", axis=0, tiled=True)
+    ways = lax.axis_size("group")
+    up = [(d, (d + 1) % ways) for d in range(ways)]
+    down = [(d, (d - 1) % ways) for d in range(ways)]
+    earlier, later = ([head_queries_dec], [head_queries_dec])
+    for __2 in range(ways // 2):
+        earlier.append(lax.ppermute(earlier[-1], "group", up))
+    for __2 in range((ways - 1) // 2):
+        later.append(lax.ppermute(later[-1], "group", down))
+    line = jnp.concatenate([*earlier[::-1], *later[1:]], axis=0)
+    all_queries = jnp.roll(
+        line, (lax.axis_index("group") - ways // 2) * head_queries_dec.shape[0], axis=0
+    )
     slots_here = dec_cache.shape[0]
     slot_local_len = dec_cache.shape[2]
     owners = lax.dynamic_slice_in_dim(slot_owner, group_rank * slots_here, slots_here)

time: 405 us -> 365 us (0.901)
  blocking collectives: 231 us -> 165 us
  starting transfers between devices: 5.69 us -> 23.2 us
  local copies, waits for them, and re-layouts: 35.3 us -> 41.9 us
    all_gather x1, blocking collectives: 84 us -> 5.25 us  [on_device(): head_queries_dec = lax.all_gather(dec_query, 'tp', axis=1, tiled=True)]
    all_gather x3, blocking collectives: 17.1 us -> 70.2 us  [merged_2(): pieces = jax.tree.map(lambda part: lax.all_gather(part, axis), value)]
    all_gather x1 -> x0, blocking collectives: 32.8 us -> none  [on_device(): all_queries = lax.all_gather(head_queries_dec, 'group', axis=0, tiled=True)]
    ppermute x0 -> x7, starting transfers between devices: none -> 14.2 us  [the longest x3 12.7 us: on_device(): later.append(lax.ppermute(later[-1], 'group', down))]
    all_to_all x1 -> x0, blocking collectives: 7.15 us -> none  [on_device(): lax.all_to_all(maxima, 'tp', split_axis=0, concat_axis=0, tiled=True)]
    dynamic_update_slice x8, local copies, waits for them, and re-layouts: 0.07 us -> 4.82 us  [on_device(): lax.map(lambda items: attend_block(items[0], items[1], items[2], visible,...]
    unnamed x25 -> x28, local copies, waits for them, and re-layouts: 18 us -> 19.1 us
  transfers between devices with their start and end apart: 2 -> 10, of which waited for: 1 -> 3; matrix products, arithmetic and copies ran while one was open for 10% -> 12% of each run, Pallas kernels for 0% -> 0%
where the time goes in v1:
time: 365 us; the launch traced here: 363 us
  blocking collectives  165 us (45%)
  matrix products  62.8 us (17%)
  local copies, waits for them, and re-layouts  41.9 us (11%)
  waiting for transfers between devices  28.5 us (8%)
  other arithmetic  27.3 us (7%)
  starting transfers between devices  23.2 us (6%)
  between operations  14.3 us (4%)
    all_gather x3, blocking collectives, merged_2(): pieces = jax.tree.map(lambda part: lax.all_gather(part, axis), value)  70.2 us
    dot_general x8, matrix products, attend_block(): jnp.einsum('gqn,nd->gqd', weights, cache_values, preferred_element_type=j...  35.8 us
    all_gather x1, blocking collectives, on_device(): lax.all_gather(head_weighted, 'group', axis=0, tiled=True)  30.6 us
    all_gather x1, blocking collectives, on_device(): lax.all_gather(head_max, 'group', axis=0, tiled=True)  26 us
    all_gather x1, blocking collectives, on_device(): lax.all_gather(head_totals, 'group', axis=0, tiled=True)  26 us
    all_gather x1, waiting for transfers between devices, on_device(): every_head = lax.all_gather(pf_query, 'tp', axis=1, tiled=True)  26 us
    dot_general x8, matrix products, attend_block(): jnp.einsum('qgd,nd->gqn', queries, cache_keys, preferred_element_type=jnp...  20.8 us
    unnamed x28, local copies, waits for them, and re-layouts  19.1 us
  transfers between devices with their start and end apart: 10, of which 3 were waited for; matrix products, arithmetic and copies ran while one was open for 12% of the time, Pallas kernels for 0%

profile of v1, /device:TPU:0, one launch (start us, length us, event | category | flops | bytes accessed | tf_op | source)
XLA Modules:
  0.0 363.4 jit_solution(15378846371170492901)
XLA Ops:
  7.2 2.3 copy.40
  9.5 4.0 %fusion.46 = (bf16[1,1,1024,1024]{3,2,1,0:T(8,128)(2,1)S(1)}, bf16[1,1,1024,1024]{3,2,1,0:T(8,128)(2,1)}) fusion(bf16[1,2,1024,1024]{3,2,1,0:T(8,128)(2,1)} %param.12), kind=kLoop, calls=%fused_computation.83 | loop fusion | bytes 8388608 | tf_op jit(solution)/shard_map/slice | solution.py:81
  13.6 3.9 %copy.61 = bf16[1,1,1024,1024]{2,3,1,0:T(8,128)(2,1)} copy(bf16[1,1,1024,1024]{3,2,1,0:T(8,128)(2,1)} %get-tuple-element.189) | data formatting | bytes 4194304
  17.5 2.6 copy.62
  20.1 0.6 dynamic_slice.45
  20.7 0.6 iota_add_fusion.2
  21.4 26.0 %all-gather.4.cloned.1.call-done = bf16[256,8192]{0,1:T(8,128)(2,1)} async-done(((bf16[256,2048]{0,1:T(8,128)(2,1)}), bf16[256,8192]{0,1:T(8,128)(2,1)}) %all-gather.4.cloned.1.call-update) | async-done | bytes 4194320 | tf_op jit(solution)/shard_map/all_gather | solution.py:78
  47.3 79.4 %while.30 = (s32[]{:T(128)}, f32[8,8,256]{2,1,0:T(8,128)}, f32[8,8,256]{2,1,0:T(8,128)S(1)}, f32[8,8,256,128]{3,2,1,0:T(8,128)}, bf16[8,1024,128]{1,2,0:T(8,128)...) while((s32[]{:T(128)}, f32[8,8,256]{2,1,0:T(8,128)}, ...), condition=%wide.region_3.4_spmd.clone, body=%wide.region_0.3_spmd.clone.sunk | while | flops 1105457152 | bytes 28384368 | solution.py:84
  47.6 2.6 fusion.59
  50.2 2.0 convert_reduce_fusion.3
  52.8 4.5 %fusion.60 = f32[8,8,256,128]{3,2,1,0:T(8,128)} fusion(f32[8,8,256,128]{3,2,1,0:T(8,128)} %get-tuple-element.319, s32[]{:T(128)S(6)} %copy.81, bf16[8,1024,128]{1,2,0:T(8,128)(2,1)} %get-tuple-element.332, f32[1024,256,8]{1,0,2:T(8,128)S(1)} %get-tuple-element.303, f32[8,256]{1,0:T(8,128)S(1)} %get-tuple-element.302, ...), kind=kOutput, calls=%fused_computation.15.clone.1 | convolution fusion | flops 547356672 | bytes 9970688 | tf_op jit(solution)/shard_map/while/body/eval_jaxpr/gqn,nd->gqd/dot_general | solution.py:31
  57.5 2.6 fusion.59
  60.1 2.0 convert_reduce_fusion.3
  62.8 4.4 %fusion.60 = f32[8,8,256,128]{3,2,1,0:T(8,128)} fusion(f32[8,8,256,128]{3,2,1,0:T(8,128)} %get-tuple-element.319, s32[]{:T(128)S(6)} %copy.81, bf16[8,1024,128]{1,2,0:T(8,128)(2,1)} %get-tuple-element.332, f32[1024,256,8]{1,0,2:T(8,128)S(1)} %get-tuple-element.303, f32[8,256]{1,0:T(8,128)S(1)} %get-tuple-element.302, ...), kind=kOutput, calls=%fused_computation.15.clone.1 | convolution fusion | flops 547356672 | bytes 9970688 | tf_op jit(solution)/shard_map/while/body/eval_jaxpr/gqn,nd->gqd/dot_general | solution.py:31
  67.4 2.6 fusion.59
  70.0 2.0 convert_reduce_fusion.3
  72.7 4.5 %fusion.60 = f32[8,8,256,128]{3,2,1,0:T(8,128)} fusion(f32[8,8,256,128]{3,2,1,0:T(8,128)} %get-tuple-element.319, s32[]{:T(128)S(6)} %copy.81, bf16[8,1024,128]{1,2,0:T(8,128)(2,1)} %get-tuple-element.332, f32[1024,256,8]{1,0,2:T(8,128)S(1)} %get-tuple-element.303, f32[8,256]{1,0:T(8,128)S(1)} %get-tuple-element.302, ...), kind=kOutput, calls=%fused_computation.15.clone.1 | convolution fusion | flops 547356672 | bytes 9970688 | tf_op jit(solution)/shard_map/while/body/eval_jaxpr/gqn,nd->gqd/dot_general | solution.py:31
  77.3 2.6 fusion.59
  79.9 2.0 convert_reduce_fusion.3
  82.6 4.5 %fusion.60 = f32[8,8,256,128]{3,2,1,0:T(8,128)} fusion(f32[8,8,256,128]{3,2,1,0:T(8,128)} %get-tuple-element.319, s32[]{:T(128)S(6)} %copy.81, bf16[8,1024,128]{1,2,0:T(8,128)(2,1)} %get-tuple-element.332, f32[1024,256,8]{1,0,2:T(8,128)S(1)} %get-tuple-element.303, f32[8,256]{1,0:T(8,128)S(1)} %get-tuple-element.302, ...), kind=kOutput, calls=%fused_computation.15.clone.1 | convolution fusion | flops 547356672 | bytes 9970688 | tf_op jit(solution)/shard_map/while/body/eval_jaxpr/gqn,nd->gqd/dot_general | solution.py:31
  87.2 2.6 fusion.59
  89.8 2.0 convert_reduce_fusion.3
  91.9 0.6 bitcast_dynamic-update-slice_fusion.3
  92.5 4.5 %fusion.60 = f32[8,8,256,128]{3,2,1,0:T(8,128)} fusion(f32[8,8,256,128]{3,2,1,0:T(8,128)} %get-tuple-element.319, s32[]{:T(128)S(6)} %copy.81, bf16[8,1024,128]{1,2,0:T(8,128)(2,1)} %get-tuple-element.332, f32[1024,256,8]{1,0,2:T(8,128)S(1)} %get-tuple-element.303, f32[8,256]{1,0:T(8,128)S(1)} %get-tuple-element.302, ...), kind=kOutput, calls=%fused_computation.15.clone.1 | convolution fusion | flops 547356672 | bytes 9970688 | tf_op jit(solution)/shard_map/while/body/eval_jaxpr/gqn,nd->gqd/dot_general | solution.py:31
  97.2 2.6 fusion.59
  99.8 2.0 convert_reduce_fusion.3
  102.4 4.5 %fusion.60 = f32[8,8,256,128]{3,2,1,0:T(8,128)} fusion(f32[8,8,256,128]{3,2,1,0:T(8,128)} %get-tuple-element.319, s32[]{:T(128)S(6)} %copy.81, bf16[8,1024,128]{1,2,0:T(8,128)(2,1)} %get-tuple-element.332, f32[1024,256,8]{1,0,2:T(8,128)S(1)} %get-tuple-element.303, f32[8,256]{1,0:T(8,128)S(1)} %get-tuple-element.302, ...), kind=kOutput, calls=%fused_computation.15.clone.1 | convolution fusion | flops 547356672 | bytes 9970688 | tf_op jit(solution)/shard_map/while/body/eval_jaxpr/gqn,nd->gqd/dot_general | solution.py:31
  107.1 2.6 fusion.59
  109.7 2.0 convert_reduce_fusion.3
  112.3 4.5 %fusion.60 = f32[8,8,256,128]{3,2,1,0:T(8,128)} fusion(f32[8,8,256,128]{3,2,1,0:T(8,128)} %get-tuple-element.319, s32[]{:T(128)S(6)} %copy.81, bf16[8,1024,128]{1,2,0:T(8,128)(2,1)} %get-tuple-element.332, f32[1024,256,8]{1,0,2:T(8,128)S(1)} %get-tuple-element.303, f32[8,256]{1,0:T(8,128)S(1)} %get-tuple-element.302, ...), kind=kOutput, calls=%fused_computation.15.clone.1 | convolution fusion | flops 547356672 | bytes 9970688 | tf_op jit(solution)/shard_map/while/body/eval_jaxpr/gqn,nd->gqd/dot_general | solution.py:31
  117.0 2.6 fusion.59
  119.6 2.0 convert_reduce_fusion.3
  122.3 4.5 %fusion.60 = f32[8,8,256,128]{3,2,1,0:T(8,128)} fusion(f32[8,8,256,128]{3,2,1,0:T(8,128)} %get-tuple-element.319, s32[]{:T(128)S(6)} %copy.81, bf16[8,1024,128]{1,2,0:T(8,128)(2,1)} %get-tuple-element.332, f32[1024,256,8]{1,0,2:T(8,128)S(1)} %get-tuple-element.303, f32[8,256]{1,0:T(8,128)S(1)} %get-tuple-element.302, ...), kind=kOutput, calls=%fused_computation.15.clone.1 | convolution fusion | flops 547356672 | bytes 9970688 | tf_op jit(solution)/shard_map/while/body/eval_jaxpr/gqn,nd->gqd/dot_general | solution.py:31
  126.7 7.1 %all_to_all.15 = f32[4,16,256]{2,1,0:T(8,128)} all-to-all(f32[4,16,256]{2,1,0:T(8,128)S(1)} %bitcast.136), channel_id=1, replica_groups=mesh['group'=8,'tp'=4] {'tp'}, dimensions={0} | all-to-all | bytes 131072 | tf_op jit(solution)/shard_map/all_to_all | solution.py:93
  133.9 3.3 all-to-all-start.1
  137.2 5.3 %all_gather.25 = bf16[2,8192]{1,0:T(2,128)(2,1)S(1)} all-gather(bf16[2,2048]{1,0:T(2,128)(2,1)S(1)} %copy-done.3), channel_id=1, replica_groups=mesh['group'=8,'tp'=4] {'tp'}, dimensions={1}, use_global_device_ids=true | all-gather | bytes 40960 | tf_op jit(solution)/shard_map/all_gather | solution.py:104
  142.4 1.5 collective-permute-start
  143.9 3.2 collective-permute-start.4
  147.2 0.6 copy-done
  147.8 5.6 %all-to-all-start = ((f32[4,16,256,128]{3,2,1,0:T(8,128)}), f32[4,16,256,128]{3,2,1,0:T(8,128)}, u32[]{:S(2)}, u32[]{:S(2)}) async-start(f32[4,16,256,128]{3,2,1,0:T(8,128)} %bitcast.129), calls=%async_computation | async-start | bytes 16777216 | tf_op jit(solution)/shard_map/all_to_all | solution.py:94
  153.6 6.9 %fusion.45 = (bf16[3,1,512,1024]{3,2,1,0:T(8,128)(2,1)}, bf16[3,1,512,1024]{3,2,1,0:T(8,128)(2,1)}) fusion(bf16[3,2,512,1024]{3,2,1,0:T(8,128)(2,1)} %param.15), kind=kLoop, calls=%fused_computation.82 | loop fusion | bytes 12582912 | tf_op jit(solution)/shard_map/slice | solution.py:125
  161.2 4.7 %collective-permute-start.5 = (bf16[2,8192]{1,0:T(2,128)(2,1)S(1)}, bf16[2,8192]{1,0:T(2,128)(2,1)S(1)}, u32[]{:S(2)}, u32[]{:S(2)}) collective-permute-start(bf16[2,8192]{1,0:T(2,128)(2,1)S(1)} %collective-permute-done.4), channel_id=1, source_target_pairs={{0,28},{4,0},{8,4},{12,8},{16,12},{20,16},{24,20},{28,24},{1,29},{... | collective-permute-start | bytes 98312 | tf_op jit(solution)/shard_map/ppermute | solution.py:112
  165.9 1.3 collective-permute-done.1
  167.8 4.7 %collective-permute-start.6 = (bf16[2,8192]{1,0:T(2,128)(2,1)S(1)}, bf16[2,8192]{1,0:T(2,128)(2,1)S(1)}, u32[]{:S(2)}, u32[]{:S(2)}) collective-permute-start(bf16[2,8192]{1,0:T(2,128)(2,1)S(1)} %collective-permute-done.5), channel_id=1, source_target_pairs={{0,28},{4,0},{8,4},{12,8},{16,12},{20,16},{24,20},{28,24},{1,29},{... | collective-permute-start | bytes 98312 | tf_op jit(solution)/shard_map/ppermute | solution.py:112
  172.5 1.3 collective-permute-done.2
  173.8 3.2 copy.63
  177.0 4.7 %copy.64 = bf16[3,1,512,1024]{2,3,0,1:T(8,128)(2,1)} copy(bf16[3,1,512,1024]{3,2,1,0:T(8,128)(2,1)} %get-tuple-element.186) | data formatting | bytes 6291456
  181.7 3.4 concatenate.6
  185.1 1.1 constant_dynamic-slice_fusion.1
  186.1 1.2 gather_fusion
  187.4 1.5 fusion.47
  189.2 58.3 %all_gather.26 = f32[4,3,64]{2,1,0:T(4,128)S(1)} all-gather(f32[1,3,64]{2,1,0:T(4,128)S(1)} %all_gather_reshape.9), channel_id=1, replica_groups=mesh['group'=8,'tp'=4] {'tp'}, dimensions={0}, use_global_device_ids=true | all-gather | bytes 3840 | tf_op jit(solution)/shard_map/all_gather | solution.py:13
  247.5 5.3 %all_gather.27 = f32[4,3,64]{2,1,0:T(4,128)S(1)} all-gather(f32[1,3,64]{2,1,0:T(4,128)S(1)} %all_gather_reshape.10), channel_id=1, replica_groups=mesh['group'=8,'tp'=4] {'tp'}, dimensions={0}, use_global_device_ids=true | all-gather | bytes 3840 | tf_op jit(solution)/shard_map/all_gather | solution.py:13
  252.9 2.8 convolution_bitcast_fusion.1
  255.7 6.5 %all_gather.28 = f32[4,3,64,128]{3,2,1,0:T(8,128)S(1)} all-gather(f32[1,3,64,128]{3,2,1,0:T(8,128)S(1)} %convolution_bitcast_fusion.1), channel_id=1, replica_groups=mesh['group'=8,'tp'=4] {'tp'}, dimensions={0}, use_global_device_ids=true | all-gather | bytes 491520 | tf_op jit(solution)/shard_map/all_gather | solution.py:13
  263.0 26.0 %all-gather.1 = f32[8,3,16]{2,1,0:T(4,128)S(1)} all-gather(f32[1,3,16]{2,1,0:T(4,128)S(1)} %dynamic-slice_bitcast_fusion), channel_id=1, replica_groups=mesh['group'=8,'tp'=4] {'group'}, dimensions={0}, use_global_device_ids=true | all-gather | bytes 1728 | tf_op jit(solution)/shard_map/all_gather | solution.py:148
  289.1 26.0 %all-gather = f32[8,3,16]{2,1,0:T(4,128)S(1)} all-gather(f32[1,3,16]{2,1,0:T(4,128)S(1)} %dynamic-slice_bitcast_fusion.1), channel_id=1, replica_groups=mesh['group'=8,'tp'=4] {'group'}, dimensions={0}, use_global_device_ids=true | all-gather | bytes 1728 | tf_op jit(solution)/shard_map/all_gather | solution.py:147
  315.2 30.6 %all_gather.29 = f32[24,16,128]{2,1,0:T(8,128)S(1)} all-gather(f32[3,16,128]{2,1,0:T(8,128)S(1)} %constant_dynamic-slice_fusion), channel_id=1, replica_groups=mesh['group'=8,'tp'=4] {'group'}, dimensions={0}, use_global_device_ids=true | all-gather | bytes 221184 | tf_op jit(solution)/shard_map/all_gather | solution.py:149
  345.8 0.7 select_reduce_fusion
  346.5 0.9 fusion.27
  347.5 1.0 fusion.20
  348.5 5.4 %multiply_reduce_fusion = f32[16,256,128]{2,1,0:T(8,128)S(1)} fusion(f32[4,16,256,128]{3,2,1,0:T(8,128)} %all-to-all-done, f32[4,16,256]{2,1,0:T(8,128)S(1)} %get-tuple-element.181), kind=kLoop, calls=%fused_computation.28 | loop fusion | flops 3670016 | bytes 10551296 | tf_op jit(solution)/shard_map/reduce_sum | solution.py:41
  353.9 0.7 fusion.16
  355.2 1.4 copy.52
  (79 shorter events, 9.7 us)
Async XLA Ops:
  7.2 40.2 %all-gather.4.cloned.1.call-start = ((), (), s32[]{:S(2)}) async-start(), calls=%async_computation.3 | async-start | bytes 5242880 | tf_op jit(solution)/shard_map/all_gather | solution.py:78
  13.6 6.6 %copy-start.6 = (s32[8]{0:T(128)S(1)}, s32[8]{0:T(128)}, u32[]{:S(2)}) copy-start(s32[8]{0:T(128)} %param.13) | copy-start | bytes 100
  47.3 89.8 %copy-start.3 = (bf16[2,2048]{1,0:T(2,128)(2,1)S(1)}, bf16[2,2048]{1,0:T(2,128)(2,1)}, u32[]{:S(2)}) copy-start(bf16[2,2048]{1,0:T(2,128)(2,1)} %param.14) | copy-start | bytes 24580
  47.3 99.8 %copy-start.7 = (s32[24]{0:T(128)S(1)}, s32[24]{0:T(128)}, u32[]{:S(2)}) copy-start(s32[24]{0:T(128)} %param.17) | copy-start | bytes 292
  133.9 13.4 %all-to-all-start.1 = ((f32[4,16,256]{2,1,0:T(8,128)}), f32[4,16,256]{2,1,0:T(8,128)S(1)}, u32[]{:S(2)}, u32[]{:S(2)}) async-start(f32[4,16,256]{2,1,0:T(8,128)} %bitcast.11), calls=%async_computation.1 | async-start | bytes 131072 | tf_op jit(solution)/shard_map/all_to_all | solution.py:92
  142.4 18.1 %collective-permute-start = (bf16[2,8192]{1,0:T(2,128)(2,1)S(1)}, bf16[2,8192]{1,0:T(2,128)(2,1)S(1)}, u32[]{:S(2)}, u32[]{:S(2)}) collective-permute-start(bf16[2,8192]{1,0:T(2,128)(2,1)S(1)} %all_gather.25), channel_id=1, source_target_pairs={{0,4},{4,8},{8,12},{12,16},{16,20},{20,24},{24,28},{28,0},{1,5},{5... | collective-permute-start | bytes 98312 | tf_op jit(solution)/shard_map/ppermute | solution.py:110
  143.9 17.3 %collective-permute-start.4 = (bf16[2,8192]{1,0:T(2,128)(2,1)S(1)}, bf16[2,8192]{1,0:T(2,128)(2,1)S(1)}, u32[]{:S(2)}, u32[]{:S(2)}) collective-permute-start(bf16[2,8192]{1,0:T(2,128)(2,1)S(1)} %all_gather.25), channel_id=1, source_target_pairs={{0,28},{4,0},{8,4},{12,8},{16,12},{20,16},{24,20},{28,24},{1,29},{... | collective-permute-start | bytes 98312 | tf_op jit(solution)/shard_map/ppermute | solution.py:112
  147.2 0.6 copy-start
  147.8 200.6 %all-to-all-start = ((f32[4,16,256,128]{3,2,1,0:T(8,128)}), f32[4,16,256,128]{3,2,1,0:T(8,128)}, u32[]{:S(2)}, u32[]{:S(2)}) async-start(f32[4,16,256,128]{3,2,1,0:T(8,128)} %bitcast.129), calls=%async_computation | async-start | bytes 16777216 | tf_op jit(solution)/shard_map/all_to_all | solution.py:94
  153.6 7.0 %copy-start.5 = (s32[24]{0:T(128)S(1)}, s32[24]{0:T(128)}, u32[]{:S(2)}) copy-start(s32[24]{0:T(128)} %param.16) | copy-start | bytes 292
  160.5 6.7 %collective-permute-start.1 = (bf16[2,8192]{1,0:T(2,128)(2,1)S(1)}, bf16[2,8192]{1,0:T(2,128)(2,1)S(1)}, u32[]{:S(2)}, u32[]{:S(2)}) collective-permute-start(bf16[2,8192]{1,0:T(2,128)(2,1)S(1)} %collective-permute-done), channel_id=1, source_target_pairs={{0,4},{4,8},{8,12},{12,16},{16,20},{20,24},{24,28},{28,0},{1,5},{5... | collective-permute-start | bytes 98312 | tf_op jit(solution)/shard_map/ppermute | solution.py:110
  161.2 6.6 %collective-permute-start.5 = (bf16[2,8192]{1,0:T(2,128)(2,1)S(1)}, bf16[2,8192]{1,0:T(2,128)(2,1)S(1)}, u32[]{:S(2)}, u32[]{:S(2)}) collective-permute-start(bf16[2,8192]{1,0:T(2,128)(2,1)S(1)} %collective-permute-done.4), channel_id=1, source_target_pairs={{0,28},{4,0},{8,4},{12,8},{16,12},{20,16},{24,20},{28,24},{1,29},{... | collective-permute-start | bytes 98312 | tf_op jit(solution)/shard_map/ppermute | solution.py:112
  167.2 6.6 %collective-permute-start.2 = (bf16[2,8192]{1,0:T(2,128)(2,1)S(1)}, bf16[2,8192]{1,0:T(2,128)(2,1)S(1)}, u32[]{:S(2)}, u32[]{:S(2)}) collective-permute-start(bf16[2,8192]{1,0:T(2,128)(2,1)S(1)} %collective-permute-done.1), channel_id=1, source_target_pairs={{0,4},{4,8},{8,12},{12,16},{16,20},{20,24},{24,28},{28,0},{1,5},{5... | collective-permute-start | bytes 98312 | tf_op jit(solution)/shard_map/ppermute | solution.py:110
  167.8 13.9 %collective-permute-start.6 = (bf16[2,8192]{1,0:T(2,128)(2,1)S(1)}, bf16[2,8192]{1,0:T(2,128)(2,1)S(1)}, u32[]{:S(2)}, u32[]{:S(2)}) collective-permute-start(bf16[2,8192]{1,0:T(2,128)(2,1)S(1)} %collective-permute-done.5), channel_id=1, source_target_pairs={{0,28},{4,0},{8,4},{12,8},{16,12},{20,16},{24,20},{28,24},{1,29},{... | collective-permute-start | bytes 98312 | tf_op jit(solution)/shard_map/ppermute | solution.py:112
  173.8 7.9 %collective-permute-start.3 = (bf16[2,8192]{1,0:T(2,128)(2,1)S(1)}, bf16[2,8192]{1,0:T(2,128)(2,1)S(1)}, u32[]{:S(2)}, u32[]{:S(2)}) collective-permute-start(bf16[2,8192]{1,0:T(2,128)(2,1)S(1)} %collective-permute-done.2), channel_id=1, source_target_pairs={{0,4},{4,8},{8,12},{12,16},{16,20},{20,24},{24,28},{28,0},{1,5},{5... | collective-permute-start | bytes 98312 | tf_op jit(solution)/shard_map/ppermute | solution.py:110
  188.9 158.6 %copy-start.4 = (pred[2,24]{1,0:T(4,128)(4,1)S(1)}, pred[2,24]{1,0:T(4,128)(4,1)}, u32[]{:S(2)}) copy-start(pred[2,24]{1,0:T(4,128)(4,1)} %broadcast_compare_fusion.2) | copy-start | bytes 148
  188.9 159.6 %copy-start.1 = (f32[4,16,256]{2,1,0:T(8,128)S(1)}, f32[4,16,256]{2,1,0:T(8,128)}, u32[]{:S(2)}) copy-start(f32[4,16,256]{2,1,0:T(8,128)} %copy-done) | copy-start | bytes 196612
  188.9 159.6 %copy-start.2 = (f32[4,16,256]{2,1,0:T(8,128)S(1)}, f32[4,16,256]{2,1,0:T(8,128)}, u32[]{:S(2)}) copy-start(f32[4,16,256]{2,1,0:T(8,128)} %all_to_all.15) | copy-start | bytes 196612
Sparse Core Ops, SparseCore 0:
  10.1 37.1 all-gather.3
